TPU v7x, 32 devices: a whole 2x2x4 slice. The times are simulated.
32 devices in a mesh: dp: 8 (over y, x, core), seq: 4 (over z).
Axes of the slice: x: 2, y: 2, z: 4, core: 2. Of those that a mesh axis runs over, the one named last changes fastest.
Arguments:
- queries: bfloat16 [8192, 1536], P(('dp', 'seq')), may hold values from -8 to 8
- keys: bfloat16 [8192, 1536], P(('dp', 'seq')), may hold values from -8 to 8
- values: bfloat16 [8192, 1536], P(('dp', 'seq')), may hold values from -6 to 6
- grad_out: bfloat16 [8192, 3072], P(('dp', 'seq')), may hold values from -2 to 2
- out_weight: bfloat16 [3072, 1536], P('dp', 'seq'), may hold values from -0.15625 to 0.15625
- clip_lengths: int32 [8, 3], P('dp'), may hold values from 1 to 512, 1024 in all within a row
Outputs:
- grad_queries: bfloat16 [8192, 1536], P(('dp', 'seq'))
- grad_keys: bfloat16 [8192, 1536], P(('dp', 'seq'))
- grad_values: bfloat16 [8192, 1536], P(('dp', 'seq'))
- grad_weight: float32 [3072, 1536], P('dp', 'seq')
Inputs may be any that keep to these rules, and one draw needn't show every extreme that they name: `clip_lengths`: each row holds 3 lengths that sum to 1024; the largest of each row is exactly 512.
All inputs are finite; a program needn't handle non-finite values.
Results may differ from a plain program's by a relative error of at most 0.012.
The roundings to bfloat16 on the way count: a program that leaves them out, or rounds other values in their place, can miss the bound.
Values may be sent and summed in bfloat16 or wider, within the bound.
A program may use at most 128 MiB of HBM per device.

v0:
```python
import jax
import jax.numpy as jnp
from jax import lax
from jax.sharding import PartitionSpec as P

HEAD_DIM = 128


def clip_index(lengths, count):
    ends = jnp.cumsum(lengths)
    positions = jnp.arange(count, dtype=jnp.int32)
    return jnp.sum((positions[:, None] >= ends[None, :]).astype(jnp.int32), axis=1)


def body(queries, keys, values, grad_out, out_weight, clip_lengths):
    head_queries, head_keys, head_values = (
        lax.all_to_all(queries, "seq", split_axis=1, concat_axis=0, tiled=True),
        lax.all_to_all(keys, "seq", split_axis=1, concat_axis=0, tiled=True),
        lax.all_to_all(values, "seq", split_axis=1, concat_axis=0, tiled=True),
    )
    group_grads = lax.all_gather(grad_out, "seq", axis=0, tiled=True)
    weight_cols = lax.all_gather(out_weight, "dp", axis=0, tiled=True)
    token_grads = jnp.dot(
        grad_out,
        lax.all_gather(weight_cols, "seq", axis=1, tiled=True),
        preferred_element_type=jnp.float32,
    ).astype(jnp.bfloat16)
    head_grads = lax.all_to_all(token_grads, "seq", split_axis=1, concat_axis=0, tiled=True)
    group_len = head_queries.shape[0]
    local_heads = head_queries.shape[1] // HEAD_DIM
    scale = HEAD_DIM ** (-0.5)
    query_heads = head_queries.reshape(group_len, local_heads, HEAD_DIM)
    key_heads = head_keys.reshape(group_len, local_heads, HEAD_DIM)
    value_heads = head_values.reshape(group_len, local_heads, HEAD_DIM)
    grad_heads = head_grads.reshape(group_len, local_heads, HEAD_DIM)
    clips = clip_index(clip_lengths[0], group_len)
    block = min(512, group_len)
    blocks = group_len // block

    def step(carry, block_index):
        key_total, value_total = carry
        start = block_index * block
        query_block = lax.dynamic_slice_in_dim(query_heads, start, block, 0)
        grad_block = lax.dynamic_slice_in_dim(grad_heads, start, block, 0)
        clip_block = lax.dynamic_slice_in_dim(clips, start, block, 0)
        scores = (
            jnp.einsum("qhd,khd->hqk", query_block, key_heads, preferred_element_type=jnp.float32)
            * scale
        )
        same_clip = clip_block[:, None] == clips[None, :]
        scores = jnp.where(same_clip[None, :, :], scores, -jnp.inf)
        top = jnp.max(scores, axis=2, keepdims=True)
        weights = jnp.exp(scores - top)
        probs = weights / jnp.sum(weights, axis=2, keepdims=True)
        probs_low = probs.astype(jnp.bfloat16)
        attention = jnp.einsum(
            "hqk,khd->qhd", probs_low, value_heads, preferred_element_type=jnp.float32
        ).astype(jnp.bfloat16)
        attention = lax.optimization_barrier(attention)
        value_total = value_total + jnp.einsum(
            "hqk,qhd->khd", probs_low, grad_block, preferred_element_type=jnp.float32
        )
        grad_probs = jnp.einsum(
            "qhd,khd->hqk", grad_block, value_heads, preferred_element_type=jnp.float32
        )
        delta = jnp.sum(grad_block.astype(jnp.float32) * attention.astype(jnp.float32), axis=2).T
        grad_scores = (probs * (grad_probs - delta[:, :, None]) * scale).astype(jnp.bfloat16)
        grad_query_block = jnp.einsum(
            "hqk,khd->qhd", grad_scores, key_heads, preferred_element_type=jnp.float32
        ).astype(jnp.bfloat16)
        key_total = key_total + jnp.einsum(
            "hqk,qhd->khd", grad_scores, query_block, preferred_element_type=jnp.float32
        )
        return ((key_total, value_total), (attention, grad_query_block))

    empty = jnp.zeros((group_len, local_heads, HEAD_DIM), jnp.float32)
    totals, outputs = lax.scan(step, (empty, empty), jnp.arange(blocks, dtype=jnp.int32))
    width = local_heads * HEAD_DIM
    attention_flat = outputs[0].reshape(group_len, width)
    grad_query_heads = outputs[1].reshape(group_len, width)
    grad_key_heads = totals[0].reshape(group_len, width).astype(jnp.bfloat16)
    grad_value_heads = totals[1].reshape(group_len, width).astype(jnp.bfloat16)
    grad_weight = lax.psum_scatter(
        lax.dot_general(
            group_grads,
            attention_flat,
            (((0,), (0,)), ((), ())),
            preferred_element_type=jnp.float32,
        ),
        "dp",
        scatter_dimension=0,
        tiled=True,
    )
    grad_queries, grad_keys, grad_values = (
        lax.all_to_all(grad_query_heads, "seq", split_axis=0, concat_axis=1, tiled=True),
        lax.all_to_all(grad_key_heads, "seq", split_axis=0, concat_axis=1, tiled=True),
        lax.all_to_all(grad_value_heads, "seq", split_axis=0, concat_axis=1, tiled=True),
    )
    return (grad_queries, grad_keys, grad_values, grad_weight)


def solution(mesh):
    placed = (
        P(("dp", "seq"), None),
        P(("dp", "seq"), None),
        P(("dp", "seq"), None),
        P(("dp", "seq"), None),
        P("dp", "seq"),
        P("dp", None),
    )
    return jax.shard_map(
        body,
        mesh=mesh,
        in_specs=placed,
        out_specs=(
            P(("dp", "seq"), None),
            P(("dp", "seq"), None),
            P(("dp", "seq"), None),
            P("dp", "seq"),
        ),
        check_vma=False,
    )
```

profile of v0, /device:TPU:0, one launch (start us, length us, event | category | flops | bytes accessed | tf_op | source)
XLA Modules:
  0.0 481.0 jit_solution(9675864120339610824)
XLA Ops:
  8.0 33.7 %all-gather.4.cloned.1.call-done = bf16[3072,384]{1,0:T(8,128)(2,1)} async-done(((bf16[384,384]{1,0:T(8,128)(2,1)}), bf16[3072,384]{1,0:T(8,128)(2,1)}) %all-gather.4.cloned.1.call-update) | async-done | bytes 2359312 | tf_op jit(solution)/shard_map/all_gather | solution.py:22
  42.9 4.6 all-to-all-start.1
  48.6 45.3 %all-to-all-done.1 = bf16[256,4,384]{0,2,1:T(8,128)(2,1)S(1)} async-done(((bf16[256,4,384]{0,2,1:T(8,128)(2,1)}), bf16[256,4,384]{0,2,1:T(8,128)(2,1)S(1)}, u32[]{:S(2)}, u32[]{:S(2)}) %all-to-all-start.1) | async-done | bytes 786464 | tf_op jit(solution)/shard_map/all_to_all | solution.py:18
  93.9 3.5 all-to-all-start.3
  98.5 46.5 %all-to-all-done.3 = bf16[256,4,384]{0,2,1:T(8,128)(2,1)S(1)} async-done(((bf16[256,4,384]{0,2,1:T(8,128)(2,1)}), bf16[256,4,384]{0,2,1:T(8,128)(2,1)S(1)}, u32[]{:S(2)}, u32[]{:S(2)}) %all-to-all-start.3) | async-done | bytes 786464 | tf_op jit(solution)/shard_map/all_to_all | solution.py:19
  145.1 3.5 all-to-all-start
  148.6 105.3 %all-gather.6.cloned.1.call-done = bf16[3072,1536]{1,0:T(8,128)(2,1)} async-done(((bf16[3072,384]{1,0:T(8,128)(2,1)}), bf16[3072,1536]{1,0:T(8,128)(2,1)}) %all-gather.6.cloned.1.call-update) | async-done | bytes 9437200 | tf_op jit(solution)/shard_map/all_gather | solution.py:25
  253.8 6.8 %convolution_convert_fusion.2 = bf16[256,1536]{1,0:T(8,128)(2,1)S(1)} fusion(bf16[256,3072]{1,0:T(8,128)(2,1)} %param.11, bf16[3072,1536]{1,0:T(8,128)(2,1)} %all-gather.6.cloned.1.call-done), kind=kOutput, calls=%fused_computation.32 | convolution fusion | flops 2416312320 | bytes 11796480 | tf_op jit(solution)/shard_map/dot_general | solution.py:23
  260.6 1.2 copy.120
  261.8 3.5 all-to-all-start.2
  266.4 1.5 copy.98
  267.9 1.8 reshape.115
  269.7 1.2 copy.104
  273.8 1.4 reshape.112
  275.3 23.1 %all-to-all-done.2 = bf16[256,4,384]{0,2,1:T(8,128)(2,1)S(1)} async-done(((bf16[256,4,384]{0,2,1:T(8,128)(2,1)}), bf16[256,4,384]{0,2,1:T(8,128)(2,1)S(1)}, u32[]{:S(2)}, u32[]{:S(2)}) %all-to-all-start.2) | async-done | bytes 786464 | tf_op jit(solution)/shard_map/all_to_all | solution.py:28
  299.0 1.5 reshape.116
  300.4 60.8 %while.17 = (s32[]{:T(128)}, f32[1024,3,128]{0,2,1:T(8,128)}, f32[1024,3,128]{0,2,1:T(8,128)}, bf16[2,512,3,128]{3,1,2,0:T(8,128)(2,1)}, bf16[2,512,3,128]{3,1,2...) while((s32[]{:T(128)}, f32[1024,3,128]{0,2,1:T(8,128)}, ...), condition=%wide.region_6.7_spmd.clone, body=%wide.region_2.6_spmd.clone.sunk | while | flops 2436496896 | bytes 93103048 | solution.py:77
  302.1 6.3 %fusion.74 = (f32[3,512]{1,0:T(4,128)S(1)}, f32[3,512,1024]{2,1,0:T(8,128)}) fusion(pred[512,1024]{1,0:T(8,128)(4,1)S(1)} %broadcast_compare_fusion.2, bf16[1024,3,128]{2,0,1:T(8,128)(2,1)} %get-tuple-element.316, bf16[1024,3,128]{0,2,1:T(8,128)(2,1)} %get-tuple-element.314, s32[]{:T(128)S(6)} %select_n.24), kind=kOutput, calls=%fused_computation.35.clone.1 | convolution fusion | flops 408945664 | bytes 8001540 | tf_op jit(solution)/shard_map/while/body/eval_jaxpr/sub | solution.py:53
  308.4 3.7 fusion.75
  312.1 1.7 fusion.76
  314.9 1.4 multiply_reduce_fusion.2
  316.3 5.2 %multiply_convert_fusion.2 = bf16[3,512,1024]{2,1,0:T(8,128)(2,1)} fusion(f32[3,512]{1,0:T(4,128)S(1)} %bitcast.114, bf16[512,3,128]{0,2,1:T(8,128)(2,1)S(1)} %constant_dynamic-slice_fusion.2, bf16[1024,3,128]{2,0,1:T(8,128)(2,1)} %get-tuple-element.318, f32[3,512,1024]{2,1,0:T(8,128)} %get-tuple-element.276, f32[3,512]{1,0:T(4,128)S(1)} %get-tuple-element.277), kind=kOutput, calls=%fused_computation.1.clone.1 | convolution fusion | flops 410517504 | bytes 10629120 | tf_op jit(solution)/shard_map/while/body/eval_jaxpr/qhd,khd->hqk/dot_general | solution.py:63
  321.5 3.9 bitcast_add_fusion.4
  325.4 2.4 fusion.77
  328.8 1.2 copy-done.3
  332.4 6.3 %fusion.74 = (f32[3,512]{1,0:T(4,128)S(1)}, f32[3,512,1024]{2,1,0:T(8,128)}) fusion(pred[512,1024]{1,0:T(8,128)(4,1)S(1)} %broadcast_compare_fusion.2, bf16[1024,3,128]{2,0,1:T(8,128)(2,1)} %get-tuple-element.316, bf16[1024,3,128]{0,2,1:T(8,128)(2,1)} %get-tuple-element.314, s32[]{:T(128)S(6)} %select_n.24), kind=kOutput, calls=%fused_computation.35.clone.1 | convolution fusion | flops 408945664 | bytes 8001540 | tf_op jit(solution)/shard_map/while/body/eval_jaxpr/sub | solution.py:53
  338.7 3.6 fusion.75
  342.3 1.7 fusion.76
  345.1 1.4 multiply_reduce_fusion.2
  346.5 5.1 %multiply_convert_fusion.2 = bf16[3,512,1024]{2,1,0:T(8,128)(2,1)} fusion(f32[3,512]{1,0:T(4,128)S(1)} %bitcast.114, bf16[512,3,128]{0,2,1:T(8,128)(2,1)S(1)} %constant_dynamic-slice_fusion.2, bf16[1024,3,128]{2,0,1:T(8,128)(2,1)} %get-tuple-element.318, f32[3,512,1024]{2,1,0:T(8,128)} %get-tuple-element.276, f32[3,512]{1,0:T(4,128)S(1)} %get-tuple-element.277), kind=kOutput, calls=%fused_computation.1.clone.1 | convolution fusion | flops 410517504 | bytes 10629120 | tf_op jit(solution)/shard_map/while/body/eval_jaxpr/qhd,khd->hqk/dot_general | solution.py:63
  351.6 4.4 bitcast_add_fusion.4
  356.0 2.3 fusion.77
  359.3 1.2 copy-done.3
  361.3 2.3 copy.113
  363.7 24.1 %all-gather.8.cloned.1.call-done = bf16[1024,3072]{1,0:T(8,128)(2,1)} async-done(((bf16[256,3072]{1,0:T(8,128)(2,1)}), bf16[1024,3072]{1,0:T(8,128)(2,1)}) %all-gather.8.cloned.1.call-update) | async-done | bytes 6291472 | tf_op jit(solution)/shard_map/all_gather | solution.py:21
  387.8 7.0 %convolution_bitcast_fusion = f32[3072,384]{0,1:T(8,128)} fusion(bf16[1024,384]{0,1:T(8,128)(2,1)S(1)} %bitcast.113, bf16[1024,3072]{1,0:T(8,128)(2,1)} %all-gather.8.cloned.1.call-done), kind=kOutput, calls=%fused_computation.31 | convolution fusion | flops 2415919104 | bytes 11796480 | tf_op jit(solution)/shard_map/dot_general | solution.py:84
  394.9 1.4 copy-done.1
  397.2 1.9 convert_element_type.47
  399.2 1.5 copy.109
  400.7 3.7 all-to-all-start.5
  405.4 2.0 convert_element_type.49
  407.5 1.5 copy.111
  409.0 15.9 %all-to-all-done.5 = bf16[4,256,384]{2,1,0:T(8,128)(2,1)S(1)} async-done(((bf16[4,256,384]{2,1,0:T(8,128)(2,1)}), bf16[4,256,384]{2,1,0:T(8,128)(2,1)S(1)}, u32[]{:S(2)}, u32[]{:S(2)}) %all-to-all-start.5) | async-done | bytes 786464 | tf_op jit(solution)/shard_map/all_to_all | solution.py:96
  424.9 3.5 all-to-all-start.6
  430.3 17.8 %all-to-all-done.6 = bf16[4,256,384]{2,1,0:T(8,128)(2,1)S(1)} async-done(((bf16[4,256,384]{2,1,0:T(8,128)(2,1)}), bf16[4,256,384]{2,1,0:T(8,128)(2,1)S(1)}, u32[]{:S(2)}, u32[]{:S(2)}) %all-to-all-start.6) | async-done | bytes 786464 | tf_op jit(solution)/shard_map/all_to_all | solution.py:97
  448.2 3.5 all-to-all-start.4
  454.5 16.7 %all-to-all-done.4 = bf16[4,256,384]{1,2,0:T(8,128)(2,1)S(1)} async-done(((bf16[4,256,384]{1,2,0:T(8,128)(2,1)}), bf16[4,256,384]{1,2,0:T(8,128)(2,1)S(1)}, u32[]{:S(2)}, u32[]{:S(2)}) %all-to-all-start.4) | async-done | bytes 786464 | tf_op jit(solution)/shard_map/all_to_all | solution.py:95
  472.4 2.1 copy.117
  (93 shorter events, 24.4 us)
Async XLA Ops:
  7.2 34.5 %copy-start.7 = (bf16[256,1536]{1,0:T(8,128)(2,1)S(1)}, bf16[256,1536]{1,0:T(8,128)(2,1)}, u32[]{:S(2)}) copy-start(bf16[256,1536]{1,0:T(8,128)(2,1)} %param.9) | copy-start | bytes 2359300
  7.2 40.3 %copy-start.8 = (bf16[256,1536]{1,0:T(8,128)(2,1)S(1)}, bf16[256,1536]{1,0:T(8,128)(2,1)}, u32[]{:S(2)}) copy-start(bf16[256,1536]{1,0:T(8,128)(2,1)} %param.10) | copy-start | bytes 2359300
  7.2 34.5 %all-gather.4.cloned.1.call-start = ((), (), s32[]{:S(2)}) async-start(), calls=%async_computation.8 | async-start | bytes 2654208 | tf_op jit(solution)/shard_map/all_gather | solution.py:22
  7.9 245.9 %all-gather.6.cloned.1.call-start = ((), (), s32[]{:S(2)}) async-start(), calls=%async_computation.9 | async-start | bytes 11796480 | tf_op jit(solution)/shard_map/all_gather | solution.py:25
  41.7 55.7 %copy-start.9 = (bf16[256,1536]{1,0:T(8,128)(2,1)S(1)}, bf16[256,1536]{1,0:T(8,128)(2,1)}, u32[]{:S(2)}) copy-start(bf16[256,1536]{1,0:T(8,128)(2,1)} %param.8) | copy-start | bytes 2359300
  42.9 51.0 %all-to-all-start.1 = ((bf16[256,4,384]{0,2,1:T(8,128)(2,1)}), bf16[256,4,384]{0,2,1:T(8,128)(2,1)S(1)}, u32[]{:S(2)}, u32[]{:S(2)}) async-start(bf16[256,4,384]{0,2,1:T(8,128)(2,1)} %bitcast.4), calls=%async_computation.1 | async-start | bytes 1572864 | tf_op jit(solution)/shard_map/all_to_all | solution.py:18
  93.9 51.2 %all-to-all-start.3 = ((bf16[256,4,384]{0,2,1:T(8,128)(2,1)}), bf16[256,4,384]{0,2,1:T(8,128)(2,1)S(1)}, u32[]{:S(2)}, u32[]{:S(2)}) async-start(bf16[256,4,384]{0,2,1:T(8,128)(2,1)} %bitcast.8), calls=%async_computation.3 | async-start | bytes 1572864 | tf_op jit(solution)/shard_map/all_to_all | solution.py:19
  145.1 116.7 %all-to-all-start = ((bf16[256,4,384]{0,2,1:T(8,128)(2,1)}), bf16[256,4,384]{0,2,1:T(8,128)(2,1)S(1)}, u32[]{:S(2)}, u32[]{:S(2)}) async-start(bf16[256,4,384]{0,2,1:T(8,128)(2,1)} %bitcast), calls=%async_computation | async-start | bytes 1572864 | tf_op jit(solution)/shard_map/all_to_all | solution.py:17
  260.6 5.5 %copy-start.14 = (s32[1,3]{1,0:T(1,128)S(1)}, s32[1,3]{1,0:T(1,128)}, u32[]{:S(2)}) copy-start(s32[1,3]{1,0:T(1,128)} %param.13) | copy-start | bytes 40
  261.8 36.6 %all-to-all-start.2 = ((bf16[256,4,384]{0,2,1:T(8,128)(2,1)}), bf16[256,4,384]{0,2,1:T(8,128)(2,1)S(1)}, u32[]{:S(2)}, u32[]{:S(2)}) async-start(bf16[256,4,384]{0,2,1:T(8,128)(2,1)} %bitcast.6), calls=%async_computation.2 | async-start | bytes 1572864 | tf_op jit(solution)/shard_map/all_to_all | solution.py:28
  265.3 122.5 %all-gather.8.cloned.1.call-start = ((), (), s32[]{:S(2)}) async-start(), calls=%async_computation.10 | async-start | bytes 7864320 | tf_op jit(solution)/shard_map/all_gather | solution.py:21
  266.0 206.4 %reduce-scatter.2.cloned.1.call-start = ((), (), s32[]{:S(2)}) async-start(), calls=%async_computation.11 | async-start | bytes 5308416 | tf_op jit(solution)/shard_map/reduce_scatter | solution.py:83
  308.4 3.7 copy-start.10
  312.1 1.8 copy-start.6
  321.5 3.9 copy-start
  321.5 3.9 copy-start.11
  325.4 2.4 copy-start.2
  327.8 0.9 copy-start.12
  327.8 2.1 copy-start.5
  328.7 1.2 copy-start.3
  338.7 3.6 copy-start.10
  342.3 1.8 copy-start.6
  351.6 4.4 copy-start
  351.6 4.4 copy-start.11
  356.0 2.4 copy-start.2
  358.3 0.9 copy-start.12
  358.4 2.1 copy-start.5
  359.3 1.2 copy-start.3
  394.8 1.4 copy-start.1
  396.2 8.2 %copy-start.4 = (f32[1024,3,128]{0,2,1:T(8,128)S(1)}, f32[1024,3,128]{0,2,1:T(8,128)}, u32[]{:S(2)}) copy-start(f32[1024,3,128]{0,2,1:T(8,128)} %get-tuple-element.66) | copy-start | bytes 4718596
  400.7 24.2 %all-to-all-start.5 = ((bf16[4,256,384]{2,1,0:T(8,128)(2,1)}), bf16[4,256,384]{2,1,0:T(8,128)(2,1)S(1)}, u32[]{:S(2)}, u32[]{:S(2)}) async-start(bf16[4,256,384]{2,1,0:T(8,128)(2,1)} %copy.109), calls=%async_computation.5 | async-start | bytes 1572864 | tf_op jit(solution)/shard_map/all_to_all | solution.py:96
  405.4 22.9 %copy-start.13 = (bf16[2,512,3,128]{3,1,2,0:T(8,128)(2,1)S(1)}, bf16[2,512,3,128]{3,1,2,0:T(8,128)(2,1)}, u32[]{:S(2)}) copy-start(bf16[2,512,3,128]{3,1,2,0:T(8,128)(2,1)} %get-tuple-element.64) | copy-start | bytes 2359300
  424.9 23.3 %all-to-all-start.6 = ((bf16[4,256,384]{2,1,0:T(8,128)(2,1)}), bf16[4,256,384]{2,1,0:T(8,128)(2,1)S(1)}, u32[]{:S(2)}, u32[]{:S(2)}) async-start(bf16[4,256,384]{2,1,0:T(8,128)(2,1)} %copy.111), calls=%async_computation.6 | async-start | bytes 1572864 | tf_op jit(solution)/shard_map/all_to_all | solution.py:97
  448.2 23.1 %all-to-all-start.4 = ((bf16[4,256,384]{1,2,0:T(8,128)(2,1)}), bf16[4,256,384]{1,2,0:T(8,128)(2,1)S(1)}, u32[]{:S(2)}, u32[]{:S(2)}) async-start(bf16[4,256,384]{1,2,0:T(8,128)(2,1)} %copy.108), calls=%async_computation.4 | async-start | bytes 1572864 | tf_op jit(solution)/shard_map/all_to_all | solution.py:95
Sparse Core Ops, SparseCore 0:
  9.9 31.7 all-gather.3
  43.2 210.5 all-gather.5
  267.7 120.0 all-gather.7
  395.0 52.0 reduce-scatter.1
where the time goes:
time: 482 us; the launch traced here: 481 us
  waiting for transfers between devices  330 us (68%)
  matrix products  55 us (11%)
  local copies, waits for them, and re-layouts  41.7 us (9%)
  starting transfers between devices  26 us (5%)
  between operations  14 us (3%)
  other arithmetic  13.1 us (3%)
    all_gather x1, waiting for transfers between devices, body(): lax.all_gather(weight_cols, 'seq', axis=1, tiled=True)  105 us
    all_to_all x1, waiting for transfers between devices, body(): lax.all_to_all(values, 'seq', split_axis=1, concat_axis=0, tiled=True)  46.5 us
    all_to_all x1, waiting for transfers between devices, body(): lax.all_to_all(keys, 'seq', split_axis=1, concat_axis=0, tiled=True)  45.3 us
    all_gather x1, waiting for transfers between devices, body(): weight_cols = lax.all_gather(out_weight, 'dp', axis=0, tiled=True)  33.7 us
    all_gather x1, waiting for transfers between devices, body(): group_grads = lax.all_gather(grad_out, 'seq', axis=0, tiled=True)  24.1 us
    all_to_all x1, waiting for transfers between devices, body(): lax.all_to_all(token_grads, 'seq', split_axis=1, concat_axis=0, tiled=True)  23.1 us
    all_to_all x1, waiting for transfers between devices, body(): lax.all_to_all(grad_value_heads, 'seq', split_axis=0, concat_axis=1, tile...  17.8 us
    all_to_all x1, waiting for transfers between devices, body(): lax.all_to_all(grad_query_heads, 'seq', split_axis=0, concat_axis=1, tile...  16.7 us
  transfers between devices with their start and end apart: 11, of which 9 were waited for; matrix products, arithmetic and copies ran while one was open for 20% of the time, Pallas kernels for 0%

commit v1 on v0

--- a/solution.py
+++ b/solution.py
@@ -20,12 +20,9 @@
     )
     group_grads = lax.all_gather(grad_out, "seq", axis=0, tiled=True)
     weight_cols = lax.all_gather(out_weight, "dp", axis=0, tiled=True)
-    token_grads = jnp.dot(
-        grad_out,
-        lax.all_gather(weight_cols, "seq", axis=1, tiled=True),
-        preferred_element_type=jnp.float32,
+    head_grads = jnp.dot(
+        group_grads, weight_cols, preferred_element_type=jnp.float32
     ).astype(jnp.bfloat16)
-    head_grads = lax.all_to_all(token_grads, "seq", split_axis=1, concat_axis=0, tiled=True)
     group_len = head_queries.shape[0]
     local_heads = head_queries.shape[1] // HEAD_DIM
     scale = HEAD_DIM ** (-0.5)
@@ -80,16 +77,16 @@
     grad_query_heads = outputs[1].reshape(group_len, width)
     grad_key_heads = totals[0].reshape(group_len, width).astype(jnp.bfloat16)
     grad_value_heads = totals[1].reshape(group_len, width).astype(jnp.bfloat16)
-    grad_weight = lax.psum_scatter(
-        lax.dot_general(
-            group_grads,
-            attention_flat,
-            (((0,), (0,)), ((), ())),
-            preferred_element_type=jnp.float32,
-        ),
-        "dp",
-        scatter_dimension=0,
-        tiled=True,
+    partial = lax.dot_general(
+        group_grads,
+        attention_flat,
+        (((0,), (0,)), ((), ())),
+        preferred_element_type=jnp.float32,
+    ).astype(jnp.bfloat16)
+    out_rows = out_weight.shape[0]
+    pieces = lax.all_to_all(partial, "dp", split_axis=0, concat_axis=0, tiled=True)
+    grad_weight = jnp.sum(
+        pieces.reshape(-1, out_rows, width).astype(jnp.float32), axis=0
     )
     grad_queries, grad_keys, grad_values = (
         lax.all_to_all(grad_query_heads, "seq", split_axis=0, concat_axis=1, tiled=True),

time: 482 us -> 354 us (0.73)
  waiting for transfers between devices: 330 us -> 192 us
  local copies, waits for them, and re-layouts: 41.7 us -> 60.9 us
  matrix products: 55 us -> 37.1 us
  starting transfers between devices: 26 us -> 34.6 us
    all_gather x1 -> x0, waiting for transfers between devices: 105 us -> none  [body(): lax.all_gather(weight_cols, 'seq', axis=1, tiled=True)]
    all_gather x1, waiting for transfers between devices: 33.7 us -> 0.01 us  [body(): weight_cols = lax.all_gather(out_weight, 'dp', axis=0, tiled=True)]
    all_gather x1, waiting for transfers between devices: 24.1 us -> 51.3 us  [body(): group_grads = lax.all_gather(grad_out, 'seq', axis=0, tiled=True)]
    all_to_all x1, waiting for transfers between devices: 46.5 us -> 24.6 us  [body(): lax.all_to_all(values, 'seq', split_axis=1, concat_axis=0, tiled=True)]
    all_to_all x1, waiting for transfers between devices: 0.01 us -> 18.9 us  [body(): lax.all_to_all(queries, 'seq', split_axis=1, concat_axis=0, tiled=True)]
    all_to_all x1, waiting for transfers between devices: 45.3 us -> 31.2 us  [body(): lax.all_to_all(keys, 'seq', split_axis=1, concat_axis=0, tiled=True)]
    all_to_all x1, waiting for transfers between devices: 17.8 us -> 9.78 us  [body(): lax.all_to_all(grad_value_heads, 'seq', split_axis=0, concat_axis=1, tile...]
    dot_general x2, matrix products: 10.4 us -> 3.87 us  [step(): jnp.einsum('qhd,khd->hqk', grad_block, value_heads, preferred_element_typ...]
  transfers between devices with their start and end apart: 11 -> 9, of which waited for: 9 -> 8; matrix products, arithmetic and copies ran while one was open for 20% -> 14% of each run, Pallas kernels for 0% -> 0%
where the time goes in v1:
time: 354 us; the launch traced here: 352 us
  waiting for transfers between devices  192 us (54%)
  local copies, waits for them, and re-layouts  60.9 us (17%)
  matrix products  37.1 us (10%)
  starting transfers between devices  34.6 us (10%)
  between operations  14.2 us (4%)
  other arithmetic  11.8 us (3%)
    all_gather x1, waiting for transfers between devices, body(): group_grads = lax.all_gather(grad_out, 'seq', axis=0, tiled=True)  51.3 us
    all_to_all x1, waiting for transfers between devices, body(): lax.all_to_all(keys, 'seq', split_axis=1, concat_axis=0, tiled=True)  31.2 us
    all_to_all x1, waiting for transfers between devices, body(): lax.all_to_all(values, 'seq', split_axis=1, concat_axis=0, tiled=True)  24.6 us
    all_to_all x1, waiting for transfers between devices, body(): lax.all_to_all(partial, 'dp', split_axis=0, concat_axis=0, tiled=True)  21.2 us
    all_to_all x1, waiting for transfers between devices, body(): lax.all_to_all(queries, 'seq', split_axis=1, concat_axis=0, tiled=True)  18.9 us
    all_to_all x1, waiting for transfers between devices, body(): lax.all_to_all(grad_key_heads, 'seq', split_axis=0, concat_axis=1, tiled=...  17.3 us
    unnamed x22, local copies, waits for them, and re-layouts  17.1 us
    all_to_all x1, waiting for transfers between devices, body(): lax.all_to_all(grad_query_heads, 'seq', split_axis=0, concat_axis=1, tile...  16.2 us
  transfers between devices with their start and end apart: 9, of which 8 were waited for; matrix products, arithmetic and copies ran while one was open for 14% of the time, Pallas kernels for 0%

profile of v1, /device:TPU:0, one launch (start us, length us, event | category | flops | bytes accessed | tf_op | source)
XLA Modules:
  0.0 352.2 jit_solution(16600095232941163069)
XLA Ops:
  8.7 2.4 copy.91
  11.0 6.3 %all-to-all-start = ((bf16[256,4,384]{0,2,1:T(8,128)(2,1)}), bf16[256,4,384]{0,2,1:T(8,128)(2,1)S(1)}, u32[]{:S(2)}, u32[]{:S(2)}) async-start(bf16[256,4,384]{0,2,1:T(8,128)(2,1)} %bitcast), calls=%async_computation | async-start | bytes 1572864 | tf_op jit(solution)/shard_map/all_to_all | solution.py:17
  18.5 18.9 %all-to-all-done = bf16[256,4,384]{0,2,1:T(8,128)(2,1)S(1)} async-done(((bf16[256,4,384]{0,2,1:T(8,128)(2,1)}), bf16[256,4,384]{0,2,1:T(8,128)(2,1)S(1)}, u32[]{:S(2)}, u32[]{:S(2)}) %all-to-all-start) | async-done | bytes 786464 | tf_op jit(solution)/shard_map/all_to_all | solution.py:17
  37.5 3.5 all-to-all-start.1
  41.0 1.2 copy.95
  42.1 31.2 %all-to-all-done.1 = bf16[256,4,384]{0,2,1:T(8,128)(2,1)S(1)} async-done(((bf16[256,4,384]{0,2,1:T(8,128)(2,1)}), bf16[256,4,384]{0,2,1:T(8,128)(2,1)S(1)}, u32[]{:S(2)}, u32[]{:S(2)}) %all-to-all-start.1) | async-done | bytes 786464 | tf_op jit(solution)/shard_map/all_to_all | solution.py:18
  73.3 9.6 %all-to-all-start.2 = ((bf16[256,4,384]{0,2,1:T(8,128)(2,1)}), bf16[256,4,384]{0,2,1:T(8,128)(2,1)}, u32[]{:S(2)}, u32[]{:S(2)}) async-start(bf16[256,4,384]{0,2,1:T(8,128)(2,1)} %bitcast.7), calls=%async_computation.2 | async-start | bytes 1572864 | tf_op jit(solution)/shard_map/all_to_all | solution.py:19
  83.2 2.6 copy.92
  85.8 2.5 reshape.112
  88.3 2.6 copy.94
  90.9 2.5 reshape.115
  93.5 2.3 copy.98
  95.8 24.6 %all-to-all-done.2 = bf16[256,4,384]{0,2,1:T(8,128)(2,1)} async-done(((bf16[256,4,384]{0,2,1:T(8,128)(2,1)}), bf16[256,4,384]{0,2,1:T(8,128)(2,1)}, u32[]{:S(2)}, u32[]{:S(2)}) %all-to-all-start.2) | async-done | bytes 786464 | tf_op jit(solution)/shard_map/all_to_all | solution.py:19
  120.4 2.6 copy.96
  123.0 2.5 reshape.117
  125.5 2.3 copy.100
  127.8 51.3 %all-gather.3.cloned.1.call-done = bf16[1024,3072]{1,0:T(8,128)(2,1)} async-done(((bf16[256,3072]{1,0:T(8,128)(2,1)}), bf16[1024,3072]{1,0:T(8,128)(2,1)}) %all-gather.3.cloned.1.call-update) | async-done | bytes 6291472 | tf_op jit(solution)/shard_map/all_gather | solution.py:21
  179.2 7.0 %convolution_convert_fusion.3 = bf16[1024,384]{0,1:T(8,128)(2,1)} fusion(bf16[1024,3072]{1,0:T(8,128)(2,1)} %all-gather.3.cloned.1.call-done, bf16[3072,384]{1,0:T(8,128)(2,1)} %all-gather.5.cloned.1.call-done), kind=kOutput, calls=%fused_computation.34 | convolution fusion | flops 2416312320 | bytes 9437184 | tf_op jit(solution)/shard_map/dot_general | solution.py:23
  186.2 44.0 %while.17 = (s32[]{:T(128)}, f32[1024,3,128]{0,2,1:T(8,128)S(1)}, f32[1024,3,128]{0,2,1:T(8,128)S(1)}, bf16[2,512,3,128]{3,1,2,0:T(8,128)(2,1)}, bf16[2,512,3,12...) while((s32[]{:T(128)}, f32[1024,3,128]{0,2,1:T(8,128)S(1)}, ...), condition=%wide.region_6.7_spmd.clone, body=%wide.region_2.6_spmd.clone.sunk | while | flops 2436496896 | bytes 96248328 | solution.py:74
  190.6 6.4 %fusion.74 = (f32[3,512]{1,0:T(4,128)S(1)}, f32[3,512,1024]{2,1,0:T(8,128)}) fusion(pred[512,1024]{1,0:T(8,128)(4,1)} %broadcast_compare_fusion.2, bf16[1024,3,128]{2,0,1:T(8,128)(2,1)} %get-tuple-element.319, bf16[1024,3,128]{0,2,1:T(8,128)(2,1)} %get-tuple-element.317, s32[]{:T(128)S(6)} %select_n.24), kind=kOutput, calls=%fused_computation.37.clone.1 | convolution fusion | flops 408945664 | bytes 8001540 | tf_op jit(solution)/shard_map/while/body/eval_jaxpr/sub | solution.py:50
  197.1 3.6 %fusion.75 = bf16[3,512,1024]{2,1,0:T(8,128)(2,1)S(1)} fusion(f32[3,512,1024]{2,1,0:T(8,128)} %get-tuple-element.279, f32[3,512]{1,0:T(4,128)S(1)} %get-tuple-element.280), kind=kLoop, calls=%fused_computation.9.clone.1 | loop fusion | flops 3145728 | bytes 9443328 | tf_op jit(solution)/shard_map/while/body/eval_jaxpr/convert_element_type | solution.py:52
  203.9 1.9 multiply_convert_fusion.2
  211.5 1.2 broadcast_compare_fusion.2
  212.6 6.4 %fusion.74 = (f32[3,512]{1,0:T(4,128)S(1)}, f32[3,512,1024]{2,1,0:T(8,128)}) fusion(pred[512,1024]{1,0:T(8,128)(4,1)} %broadcast_compare_fusion.2, bf16[1024,3,128]{2,0,1:T(8,128)(2,1)} %get-tuple-element.319, bf16[1024,3,128]{0,2,1:T(8,128)(2,1)} %get-tuple-element.317, s32[]{:T(128)S(6)} %select_n.24), kind=kOutput, calls=%fused_computation.37.clone.1 | convolution fusion | flops 408945664 | bytes 8001540 | tf_op jit(solution)/shard_map/while/body/eval_jaxpr/sub | solution.py:50
  219.1 3.6 %fusion.75 = bf16[3,512,1024]{2,1,0:T(8,128)(2,1)S(1)} fusion(f32[3,512,1024]{2,1,0:T(8,128)} %get-tuple-element.279, f32[3,512]{1,0:T(4,128)S(1)} %get-tuple-element.280), kind=kLoop, calls=%fused_computation.9.clone.1 | loop fusion | flops 3145728 | bytes 9443328 | tf_op jit(solution)/shard_map/while/body/eval_jaxpr/convert_element_type | solution.py:52
  225.9 1.9 multiply_convert_fusion.2
  230.2 3.1 copy.101
  233.3 3.3 all_to_all.89
  236.6 2.1 copy.102
  238.7 4.2 %all-to-all-start.3 = ((bf16[4,256,384]{1,2,0:T(8,128)(2,1)}), bf16[4,256,384]{1,2,0:T(8,128)(2,1)}, u32[]{:S(2)}, u32[]{:S(2)}) async-start(bf16[4,256,384]{1,2,0:T(8,128)(2,1)} %copy.102), calls=%async_computation.3 | async-start | bytes 1572864 | tf_op jit(solution)/shard_map/all_to_all | solution.py:92
  243.9 1.9 convert_element_type.56
  245.9 1.5 copy.103
  247.4 16.2 %all-to-all-done.3 = bf16[4,256,384]{1,2,0:T(8,128)(2,1)} async-done(((bf16[4,256,384]{1,2,0:T(8,128)(2,1)}), bf16[4,256,384]{1,2,0:T(8,128)(2,1)}, u32[]{:S(2)}, u32[]{:S(2)}) %all-to-all-start.3) | async-done | bytes 786464 | tf_op jit(solution)/shard_map/all_to_all | solution.py:92
  263.6 3.7 %all-to-all-start.4 = ((bf16[4,256,384]{2,1,0:T(8,128)(2,1)}), bf16[4,256,384]{2,1,0:T(8,128)(2,1)S(1)}, u32[]{:S(2)}, u32[]{:S(2)}) async-start(bf16[4,256,384]{2,1,0:T(8,128)(2,1)} %copy.103), calls=%async_computation.4 | async-start | bytes 1572864 | tf_op jit(solution)/shard_map/all_to_all | solution.py:93
  268.0 1.5 copy.105
  269.5 17.3 %all-to-all-done.4 = bf16[4,256,384]{2,1,0:T(8,128)(2,1)S(1)} async-done(((bf16[4,256,384]{2,1,0:T(8,128)(2,1)}), bf16[4,256,384]{2,1,0:T(8,128)(2,1)S(1)}, u32[]{:S(2)}, u32[]{:S(2)}) %all-to-all-start.4) | async-done | bytes 786464 | tf_op jit(solution)/shard_map/all_to_all | solution.py:93
  286.8 3.5 all-to-all-start.5
  290.3 2.3 copy.107
  292.8 5.6 %convolution_convert_fusion.2 = bf16[384,3072]{1,0:T(8,128)(2,1)S(1)} fusion(bf16[1024,384]{0,1:T(8,128)(2,1)S(1)} %bitcast.114, bf16[1024,3072]{1,0:T(8,128)(2,1)} %all-gather.3.cloned.1.call-done), kind=kOutput, calls=%fused_computation.32 | convolution fusion | flops 2417098752 | bytes 9437184 | tf_op jit(solution)/shard_map/dot_general | solution.py:80
  298.4 1.7 copy.122
  300.1 9.8 %all-to-all-done.5 = bf16[4,256,384]{2,1,0:T(8,128)(2,1)S(1)} async-done(((bf16[4,256,384]{2,1,0:T(8,128)(2,1)}), bf16[4,256,384]{2,1,0:T(8,128)(2,1)S(1)}, u32[]{:S(2)}, u32[]{:S(2)}) %all-to-all-start.5) | async-done | bytes 786464 | tf_op jit(solution)/shard_map/all_to_all | solution.py:94
  310.8 3.7 %all-to-all-start.6 = ((bf16[8,384,384]{1,2,0:T(8,128)(2,1)}), bf16[8,384,384]{1,2,0:T(8,128)(2,1)S(1)}, u32[]{:S(2)}, u32[]{:S(2)}) async-start(bf16[8,384,384]{1,2,0:T(8,128)(2,1)} %bitcast.70), calls=%async_computation.6 | async-start | bytes 4718592 | tf_op jit(solution)/shard_map/all_to_all | solution.py:87
  314.5 2.3 copy.110
  316.8 1.2 copy.104
  318.0 2.3 copy.111
  320.3 1.4 copy.106
  321.7 1.2 copy.112
  322.8 21.2 %all-to-all-done.6 = bf16[8,384,384]{1,2,0:T(8,128)(2,1)S(1)} async-done(((bf16[8,384,384]{1,2,0:T(8,128)(2,1)}), bf16[8,384,384]{1,2,0:T(8,128)(2,1)S(1)}, u32[]{:S(2)}, u32[]{:S(2)}) %all-to-all-start.6) | async-done | bytes 2359328 | tf_op jit(solution)/shard_map/all_to_all | solution.py:87
  (94 shorter events, 24.2 us)
Async XLA Ops:
  7.2 10.2 %copy-start.5 = (bf16[256,1536]{1,0:T(8,128)(2,1)S(1)}, bf16[256,1536]{1,0:T(8,128)(2,1)}, u32[]{:S(2)}) copy-start(bf16[256,1536]{1,0:T(8,128)(2,1)} %param.9) | copy-start | bytes 2359300
  7.2 120.7 %all-gather.5.cloned.1.call-start = ((), (), s32[]{:S(2)}) async-start(), calls=%async_computation.8 | async-start | bytes 2654208 | tf_op jit(solution)/shard_map/all_gather | solution.py:22
  7.9 171.2 %all-gather.3.cloned.1.call-start = ((), (), s32[]{:S(2)}) async-start(), calls=%async_computation.7 | async-start | bytes 7864320 | tf_op jit(solution)/shard_map/all_gather | solution.py:21
  8.7 32.3 %copy-start.6 = (bf16[256,1536]{1,0:T(8,128)(2,1)S(1)}, bf16[256,1536]{1,0:T(8,128)(2,1)}, u32[]{:S(2)}) copy-start(bf16[256,1536]{1,0:T(8,128)(2,1)} %param.10) | copy-start | bytes 2359300
  11.0 26.4 %all-to-all-start = ((bf16[256,4,384]{0,2,1:T(8,128)(2,1)}), bf16[256,4,384]{0,2,1:T(8,128)(2,1)S(1)}, u32[]{:S(2)}, u32[]{:S(2)}) async-start(bf16[256,4,384]{0,2,1:T(8,128)(2,1)} %bitcast), calls=%async_computation | async-start | bytes 1572864 | tf_op jit(solution)/shard_map/all_to_all | solution.py:17
  17.3 65.6 %copy-start.13 = (s32[1,3]{1,0:T(1,128)S(1)}, s32[1,3]{1,0:T(1,128)}, u32[]{:S(2)}) copy-start(s32[1,3]{1,0:T(1,128)} %param.13) | copy-start | bytes 40
  37.5 45.4 %copy-start.2 = (bf16[256,4,384]{0,2,1:T(8,128)(2,1)}, bf16[256,4,384]{0,2,1:T(8,128)(2,1)S(1)}, u32[]{:S(2)}) copy-start(bf16[256,4,384]{0,2,1:T(8,128)(2,1)S(1)} %all-to-all-done) | copy-start | bytes 2359300
  37.5 35.9 %all-to-all-start.1 = ((bf16[256,4,384]{0,2,1:T(8,128)(2,1)}), bf16[256,4,384]{0,2,1:T(8,128)(2,1)S(1)}, u32[]{:S(2)}, u32[]{:S(2)}) async-start(bf16[256,4,384]{0,2,1:T(8,128)(2,1)} %bitcast.4), calls=%async_computation.1 | async-start | bytes 1572864 | tf_op jit(solution)/shard_map/all_to_all | solution.py:18
  73.3 9.6 %copy-start.4 = (bf16[256,4,384]{0,2,1:T(8,128)(2,1)}, bf16[256,4,384]{0,2,1:T(8,128)(2,1)S(1)}, u32[]{:S(2)}) copy-start(bf16[256,4,384]{0,2,1:T(8,128)(2,1)S(1)} %all-to-all-done.1) | copy-start | bytes 2359300
  73.3 47.1 %all-to-all-start.2 = ((bf16[256,4,384]{0,2,1:T(8,128)(2,1)}), bf16[256,4,384]{0,2,1:T(8,128)(2,1)}, u32[]{:S(2)}, u32[]{:S(2)}) async-start(bf16[256,4,384]{0,2,1:T(8,128)(2,1)} %bitcast.7), calls=%async_computation.2 | async-start | bytes 1572864 | tf_op jit(solution)/shard_map/all_to_all | solution.py:19
  197.1 3.6 %copy-start.8 = (bf16[1024,3,128]{2,0,1:T(8,128)(2,1)S(1)}, bf16[1024,3,128]{2,0,1:T(8,128)(2,1)}, u32[]{:S(2)}) copy-start(bf16[1024,3,128]{2,0,1:T(8,128)(2,1)} %get-tuple-element.321) | copy-start | bytes 2359300 | tf_op jit(solution)/shard_map/while
  200.7 2.5 slice-start
  201.7 1.3 copy-start
  201.7 2.2 slice-start.1
  203.9 2.0 copy-start.11
  203.9 2.0 copy-start.7
  203.9 2.0 copy-start.9
  205.9 1.4 copy-start.1
  206.0 2.2 copy-start.12
  207.3 0.9 copy-start.10
  219.1 3.6 %copy-start.8 = (bf16[1024,3,128]{2,0,1:T(8,128)(2,1)S(1)}, bf16[1024,3,128]{2,0,1:T(8,128)(2,1)}, u32[]{:S(2)}) copy-start(bf16[1024,3,128]{2,0,1:T(8,128)(2,1)} %get-tuple-element.321) | copy-start | bytes 2359300 | tf_op jit(solution)/shard_map/while
  222.7 2.5 slice-start
  223.7 1.3 copy-start
  223.7 2.2 slice-start.1
  225.9 2.0 copy-start.11
  225.9 2.0 copy-start.7
  225.9 2.0 copy-start.9
  227.9 1.4 copy-start.1
  228.0 2.2 copy-start.12
  229.3 0.9 copy-start.10
  238.7 24.9 %all-to-all-start.3 = ((bf16[4,256,384]{1,2,0:T(8,128)(2,1)}), bf16[4,256,384]{1,2,0:T(8,128)(2,1)}, u32[]{:S(2)}, u32[]{:S(2)}) async-start(bf16[4,256,384]{1,2,0:T(8,128)(2,1)} %copy.102), calls=%async_computation.3 | async-start | bytes 1572864 | tf_op jit(solution)/shard_map/all_to_all | solution.py:92
  263.6 23.2 %all-to-all-start.4 = ((bf16[4,256,384]{2,1,0:T(8,128)(2,1)}), bf16[4,256,384]{2,1,0:T(8,128)(2,1)S(1)}, u32[]{:S(2)}, u32[]{:S(2)}) async-start(bf16[4,256,384]{2,1,0:T(8,128)(2,1)} %copy.103), calls=%async_computation.4 | async-start | bytes 1572864 | tf_op jit(solution)/shard_map/all_to_all | solution.py:93
  286.8 23.1 %all-to-all-start.5 = ((bf16[4,256,384]{2,1,0:T(8,128)(2,1)}), bf16[4,256,384]{2,1,0:T(8,128)(2,1)S(1)}, u32[]{:S(2)}, u32[]{:S(2)}) async-start(bf16[4,256,384]{2,1,0:T(8,128)(2,1)} %copy.105), calls=%async_computation.5 | async-start | bytes 1572864 | tf_op jit(solution)/shard_map/all_to_all | solution.py:94
  309.9 0.9 copy-start.3
  310.8 33.2 %all-to-all-start.6 = ((bf16[8,384,384]{1,2,0:T(8,128)(2,1)}), bf16[8,384,384]{1,2,0:T(8,128)(2,1)S(1)}, u32[]{:S(2)}, u32[]{:S(2)}) async-start(bf16[8,384,384]{1,2,0:T(8,128)(2,1)} %bitcast.70), calls=%async_computation.6 | async-start | bytes 4718592 | tf_op jit(solution)/shard_map/all_to_all | solution.py:87
Sparse Core Ops, SparseCore 0:
  9.9 31.7 all-gather.4
  43.2 135.8 all-gather.2

commit v2 on v1

v2 whole, which is shorter than its diff:
```python
import functools

import jax
import jax.numpy as jnp
from jax import lax
from jax.experimental import pallas as pl
from jax.experimental.pallas import tpu as pltpu
from jax.sharding import PartitionSpec as P

HEAD_DIM = 128
MESH = pl.DeviceIdType.MESH


def mul(a, b, da, db):
    return lax.dot_general(a, b, (((da,), (db,)), ((), ())), preferred_element_type=jnp.float32)


def kernel(n_dp, n_seq, q, k, v, go, w, cl, gq, gk, gv, gw,
           hq, hk, hv, gg, wc, oq, ok, ov, gk_acc, gv_acc, gw_acc, part, recv, att, ga,
           s_in, r_in, s_w, r_w, s_left, s_right, r_g, s_out, r_out, s_p, r_p, s_own):
    dp, me = lax.axis_index("dp"), lax.axis_index("seq")
    tok = q.shape[0]
    group = tok * n_seq
    width = hq.shape[1]
    heads = width // HEAD_DIM
    wrows = w.shape[0]
    d_out = go.shape[1]
    scale = HEAD_DIM ** (-0.5)

    def toks(i):
        return pl.ds(pl.multiple_of(i * tok, tok), tok)

    def cols(i):
        return pl.ds(pl.multiple_of(i * width, width), width)

    def feats(i):
        return pl.ds(pl.multiple_of(i * wrows, wrows), wrows)

    def remote(src, dst, ssem, rsem, **device):
        return pltpu.make_async_remote_copy(
            src_ref=src, dst_ref=dst, send_sem=ssem, recv_sem=rsem,
            device_id=device, device_id_type=MESH)

    barrier = pltpu.get_barrier_semaphore()
    for d in range(1, n_seq):
        pl.semaphore_signal(barrier, inc=1, device_id={"seq": lax.rem(me + d, n_seq)}, device_id_type=MESH)

    @pl.loop(1, n_dp)
    def _(d):
        pl.semaphore_signal(barrier, inc=1, device_id={"dp": lax.rem(dp + d, n_dp)}, device_id_type=MESH)

    own = [
        pltpu.make_async_copy(q.at[:, cols(me)], hq.at[toks(me), :], s_own.at[0]),
        pltpu.make_async_copy(k.at[:, cols(me)], hk.at[toks(me), :], s_own.at[1]),
        pltpu.make_async_copy(v.at[:, cols(me)], hv.at[toks(me), :], s_own.at[2]),
        pltpu.make_async_copy(go, gg.at[me], s_own.at[3]),
        pltpu.make_async_copy(w, wc.at[feats(dp), :], s_own.at[4]),
    ]
    for c in own:
        c.start()
    pl.semaphore_wait(barrier, n_seq - 1 + n_dp - 1)

    def exchange(i, src, dst, frm, to):
        return remote(src.at[:, cols(to)], dst.at[toks(frm), :], s_in.at[i, to], r_in.at[i, frm], seq=to)

    def to_right(b):
        src = gg.at[b]
        return remote(src, gg.at[b], s_right.at[b], r_g.at[b], seq=lax.rem(me + 1, n_seq))

    def to_left(b):
        return remote(gg.at[b], gg.at[b], s_left.at[b], r_g.at[b], seq=lax.rem(me + n_seq - 1, n_seq))

    def weight(frm, to):
        return remote(w, wc.at[feats(frm), :], s_w.at[to], r_w.at[frm], dp=to)

    pairs = ((q, hq), (k, hk), (v, hv))
    own[3].wait()

    @pl.when(me < n_seq - 1)
    def _():
        to_right(me).start()

    @pl.when(me > 0)
    def _():
        to_left(me).start()

    for d in range(1, n_seq):
        to = lax.rem(me + d, n_seq)
        for i, (src, dst) in enumerate(pairs):
            exchange(i, src, dst, me, to).start()

    @pl.loop(1, n_dp)
    def _(d):
        weight(dp, lax.rem(dp + d, n_dp)).start()

    gk_acc[...] = jnp.zeros_like(gk_acc)
    gv_acc[...] = jnp.zeros_like(gv_acc)
    gw_acc[...] = jnp.zeros_like(gw_acc)
    for i in (0, 1, 2, 4):
        own[i].wait()

    @pl.loop(1, n_dp)
    def _(d):
        frm = lax.rem(dp + d, n_dp)
        weight(frm, frm).wait_recv()

    for d in range(1, n_seq):
        frm = lax.rem(me + d, n_seq)
        for i, (src, dst) in enumerate(pairs):
            exchange(i, src, dst, frm, frm).wait_recv()

    def clip_of(positions):
        index, end = jnp.zeros_like(positions), 0
        for c in range(cl.shape[1]):
            end = end + cl[0, c]
            index = index + jnp.where(positions >= end, 1, 0)
        return index

    def returned(i, src, dst, frm, to):
        return remote(src.at[toks(to), :], dst.at[:, cols(frm)], s_out.at[i, to], r_out.at[i, frm], seq=to)

    def work(b):
        ga[...] = mul(gg[b], wc[...], 1, 0).astype(jnp.bfloat16)
        same = (clip_of(lax.broadcasted_iota(jnp.int32, (tok, 1), 0) + b * tok)
                == clip_of(lax.broadcasted_iota(jnp.int32, (1, group), 1)))
        for h in range(heads):
            c = slice(h * HEAD_DIM, (h + 1) * HEAD_DIM)
            qh, gh = hq[toks(b), c], ga[:, c]
            kh, vh = hk[:, c], hv[:, c]
            scores = jnp.where(same, mul(qh, kh, 1, 1) * scale, -jnp.inf)
            top = jnp.max(scores, axis=1, keepdims=True)
            weights = jnp.exp(scores - top)
            probs = weights * (1.0 / jnp.sum(weights, axis=1, keepdims=True))
            low = probs.astype(jnp.bfloat16)
            ah = mul(low, vh, 1, 0).astype(jnp.bfloat16)
            att[:, c] = ah
            gv_acc[:, c] += mul(low, gh, 0, 0)
            delta = jnp.sum(gh.astype(jnp.float32) * ah.astype(jnp.float32), axis=1, keepdims=True)
            gs = (probs * (mul(gh, vh, 1, 1) - delta) * scale).astype(jnp.bfloat16)
            oq[toks(b), c] = mul(gs, kh, 1, 0).astype(jnp.bfloat16)
            gk_acc[:, c] += mul(gs, qh, 0, 0)
        step = min(512, d_out)
        for f in range(0, d_out, step):
            gw_acc[f:f + step, :] += mul(gg[b, :, f:f + step], att[...], 0, 0)

    @pl.loop(0, 2 * n_seq - 1)
    def _(j):
        s, side = (j + 1) // 2, j % 2
        b = jnp.where(side == 1, me - s, me + s)

        @pl.when((b >= 0) & (b < n_seq))
        def _():
            @pl.when(b < me)
            def _():
                to_right(b).wait_recv()

                @pl.when(me < n_seq - 1)
                def _():
                    to_right(b).start()

            @pl.when(b > me)
            def _():
                to_left(b).wait_recv()

                @pl.when(me > 0)
                def _():
                    to_left(b).start()

            work(b)

            @pl.when(b != me)
            def _():
                returned(0, oq, gq, me, b).start()

    ok[...] = gk_acc[...].astype(jnp.bfloat16)
    ov[...] = gv_acc[...].astype(jnp.bfloat16)
    for d in range(1, n_seq):
        to = lax.rem(me + d, n_seq)
        returned(1, ok, gk, me, to).start()
        returned(2, ov, gv, me, to).start()
    part[...] = gw_acc[...].astype(jnp.bfloat16)

    def partial(frm, to):
        return remote(part.at[feats(to), :], recv.at[frm], s_p.at[to], r_p.at[frm], dp=to)

    @pl.loop(1, n_dp)
    def _(d):
        partial(dp, lax.rem(dp + d, n_dp)).start()

    kept = [
        pltpu.make_async_copy(oq.at[toks(me), :], gq.at[:, cols(me)], s_own.at[0]),
        pltpu.make_async_copy(ok.at[toks(me), :], gk.at[:, cols(me)], s_own.at[1]),
        pltpu.make_async_copy(ov.at[toks(me), :], gv.at[:, cols(me)], s_own.at[2]),
    ]
    for c in kept:
        c.start()
    gw[...] = gw_acc[feats(dp), :]

    @pl.loop(1, n_dp)
    def _(d):
        frm = lax.rem(dp + n_dp - d, n_dp)
        partial(frm, frm).wait_recv()
        gw[...] += recv[frm].astype(jnp.float32)

    for c in kept:
        c.wait()
    for d in range(1, n_seq):
        frm = lax.rem(me + d, n_seq)
        for i, (src, dst) in enumerate(((oq, gq), (ok, gk), (ov, gv))):
            returned(i, src, dst, frm, frm).wait_recv()
            returned(i, src, dst, me, frm).wait_send()
        for i, (src, dst) in enumerate(pairs):
            exchange(i, src, dst, me, frm).wait_send()

    @pl.loop(1, n_dp)
    def _(d):
        to = lax.rem(dp + d, n_dp)
        weight(dp, to).wait_send()
        partial(dp, to).wait_send()

    @pl.loop(0, n_seq)
    def _(b):
        @pl.when((b <= me) & (me < n_seq - 1))
        def _():
            to_right(b).wait_send()

        @pl.when((b >= me) & (me > 0))
        def _():
            to_left(b).wait_send()


def body(n_dp, n_seq, queries, keys, values, grad_out, out_weight, clip_lengths):
    tok, all_width = queries.shape
    d_out = grad_out.shape[1]
    wrows, width = out_weight.shape
    group = tok * n_seq
    bf, f32 = jnp.bfloat16, jnp.float32
    vmem = pl.BlockSpec(memory_space=pltpu.VMEM)
    dma = pltpu.SemaphoreType.DMA
    return tuple(pl.pallas_call(
        functools.partial(kernel, n_dp, n_seq),
        out_shape=(jax.ShapeDtypeStruct((tok, all_width), bf),) * 3
        + (jax.ShapeDtypeStruct((wrows, width), f32),),
        in_specs=[vmem] * 5 + [pl.BlockSpec(memory_space=pltpu.SMEM)],
        out_specs=(vmem,) * 4,
        scratch_shapes=[pltpu.VMEM((group, width), bf)] * 3
        + [pltpu.VMEM((n_seq, tok, d_out), bf), pltpu.VMEM((d_out, width), bf)]
        + [pltpu.VMEM((group, width), bf)] * 3
        + [pltpu.VMEM((group, width), f32)] * 2
        + [pltpu.VMEM((d_out, width), f32), pltpu.VMEM((d_out, width), bf),
           pltpu.VMEM((n_dp, wrows, width), bf),
           pltpu.VMEM((tok, width), bf), pltpu.VMEM((tok, width), bf)]
        + [dma((3, n_seq)), dma((3, n_seq)), dma((n_dp,)), dma((n_dp,)),
           dma((n_seq,)), dma((n_seq,)), dma((n_seq,)),
           dma((3, n_seq)), dma((3, n_seq)), dma((n_dp,)), dma((n_dp,)), dma((5,))],
        compiler_params=pltpu.CompilerParams(
            collective_id=0, has_side_effects=True, vmem_limit_bytes=56 * 1024 * 1024),
        cost_estimate=pl.CostEstimate(
            flops=2 * group * width * (2 * d_out + 6 * group),
            bytes_accessed=16 * tok * all_width, transcendentals=group * group * width // HEAD_DIM),
    )(queries, keys, values, grad_out, out_weight, clip_lengths))


def solution(mesh):
    placed = (
        P(("dp", "seq"), None),
        P(("dp", "seq"), None),
        P(("dp", "seq"), None),
        P(("dp", "seq"), None),
        P("dp", "seq"),
        P("dp", None),
    )
    return jax.shard_map(
        functools.partial(body, mesh.shape["dp"], mesh.shape["seq"]),
        mesh=mesh,
        in_specs=placed,
        out_specs=(
            P(("dp", "seq"), None),
            P(("dp", "seq"), None),
            P(("dp", "seq"), None),
            P("dp", "seq"),
        ),
        check_vma=False,
    )
```

time: 354 us -> 242 us (0.68)
  Pallas kernels: 0 us -> 236 us
  waiting for transfers between devices: 192 us -> 0 us
  local copies, waits for them, and re-layouts: 60.9 us -> 4.77 us
  matrix products: 37.1 us -> 0 us
  starting transfers between devices: 34.6 us -> 0 us
  between operations: 14.2 us -> 0.66 us
  other arithmetic: 11.8 us -> 0 us
    pallas_call x0 -> x1, Pallas kernels: none -> 236 us  [body(): pl.pallas_call(functools.partial(kernel, n_dp, n_seq), out_shape=(jax.Sha...]
    all_to_all x7 -> x0, waiting for transfers between devices: 139 us -> none  [the longest x1 31.2 us: body(): lax.all_to_all(keys, 'seq', split_axis=1, concat_axis=0, tiled=True)]
    all_gather x2 -> x0, waiting for transfers between devices: 51.3 us -> none  [the longest x1 51.3 us: body(): group_grads = lax.all_gather(grad_out, 'seq', axis=0, tiled=True)]
    all_to_all x7 -> x0, starting transfers between devices: 34.5 us -> none  [the longest x1 9.57 us: body(): lax.all_to_all(values, 'seq', split_axis=1, concat_axis=0, tiled=True)]
    dot_general x12 -> x0, matrix products: 24.3 us -> none  [the longest x1 7.04 us: body(): jnp.dot(group_grads, weight_cols, preferred_element_type=jnp.float32)]
    all_to_all x8 -> x0, local copies, waits for them, and re-layouts: 17.6 us -> none  [the longest x2 5.44 us: body(): lax.all_to_all(grad_query_heads, 'seq', split_axis=0, concat_axis=1, tile...]
    sub x2 -> x0, matrix products: 12.8 us -> none  [step(): weights = jnp.exp(scores - top)]
    unnamed x22 -> x10, local copies, waits for them, and re-layouts: 17.1 us -> 4.77 us
  transfers between devices with their start and end apart: 9 -> 0, of which waited for: 8 -> 0; matrix products, arithmetic and copies ran while one was open for 14% -> 0% of each run, Pallas kernels for 0% -> 0%
where the time goes in v2:
time: 242 us; the launch traced here: 241 us
  Pallas kernels  236 us (98%)
  local copies, waits for them, and re-layouts  4.77 us (2%)
    pallas_call x1, Pallas kernels, body(): pl.pallas_call(functools.partial(kernel, n_dp, n_seq), out_shape=(jax.Sha...  236 us

profile of v2, /device:TPU:0, one launch (start us, length us, event | category | flops | bytes accessed | tf_op | source)
XLA Modules:
  0.0 241.5 jit_solution(11927173145640499153)
XLA Ops:
  0.6 236.0 %shard_map.93 = (bf16[256,1536]{1,0:T(8,128)(2,1)}, bf16[256,1536]{1,0:T(8,128)(2,1)}, bf16[256,1536]{1,0:T(8,128)(2,1)}, f32[384,384]{1,0:T(8,128)}) custom-call(bf16[256,1536]{1,0:T(8,128)(2,1)} %q.1, bf16[256,1536]{1,0:T(8,128)(2,1)} %k.1, bf16[256,1536]{1,0:T(8,128)(2,1)} %v.1, bf16[256,3072]{1,0:T(8,128)(2,1)} %go.1, bf16[384,384]{1,0:T(8,128)(2,1)} %w.1, ...), custom_call_target="tpu_custom_call" | custom-call | flops 9663676416 | bytes 6291456 | tf_op jit(solution)/shard_map/pallas_call | solution.py:240
  236.7 0.0 copy-start.1
  236.7 0.0 copy-start
  236.7 2.2 copy.14
  238.9 0.0 copy-done.1
  238.9 0.0 copy-start.2
  238.9 0.9 copy.15
  239.8 0.0 copy-done
  239.8 0.9 copy.16
  240.7 0.0 copy-done.2
  240.7 0.8 copy.17
Async XLA Ops:
  236.7 2.2 copy-start.1
  236.7 3.1 %copy-start = (bf16[256,1536]{1,0:T(8,128)(2,1)S(1)}, bf16[256,1536]{1,0:T(8,128)(2,1)}, u32[]{:S(2)}) copy-start(bf16[256,1536]{1,0:T(8,128)(2,1)} %get-tuple-element.10) | copy-start | bytes 2359300
  238.9 1.8 copy-start.2

commit v3 on v2

--- a/solution.py
+++ b/solution.py
@@ -93,11 +93,31 @@
     def _(d):
         weight(dp, lax.rem(dp + d, n_dp)).start()
 
+    def turn(j):
+        s = (j + 1) // 2
+        return jnp.where(j % 2 == 1, me - s, me + s)
+
+    def relay(j):
+        b = turn(j)
+
+        @pl.when((b >= 0) & (b < me) & (me < n_seq - 1))
+        def _():
+            to_right(b).wait_recv()
+            to_right(b).start()
+
+        @pl.when((b > me) & (b < n_seq) & (me > 0))
+        def _():
+            to_left(b).wait_recv()
+            to_left(b).start()
+
     gk_acc[...] = jnp.zeros_like(gk_acc)
     gv_acc[...] = jnp.zeros_like(gv_acc)
     gw_acc[...] = jnp.zeros_like(gw_acc)
     for i in (0, 1, 2, 4):
         own[i].wait()
+
+    relay(1)
+    relay(2)
 
     @pl.loop(1, n_dp)
     def _(d):
@@ -145,26 +165,22 @@
 
     @pl.loop(0, 2 * n_seq - 1)
     def _(j):
-        s, side = (j + 1) // 2, j % 2
-        b = jnp.where(side == 1, me - s, me + s)
+        @pl.when((j % 2 == 0) & (j >= 2))
+        def _():
+            relay(j + 1)
+            relay(j + 2)
+
+        b = turn(j)
 
         @pl.when((b >= 0) & (b < n_seq))
         def _():
-            @pl.when(b < me)
+            @pl.when((b < me) & (me == n_seq - 1))
             def _():
                 to_right(b).wait_recv()
 
-                @pl.when(me < n_seq - 1)
-                def _():
-                    to_right(b).start()
-
-            @pl.when(b > me)
+            @pl.when((b > me) & (me == 0))
             def _():
                 to_left(b).wait_recv()
-
-                @pl.when(me > 0)
-                def _():
-                    to_left(b).start()
 
             work(b)
 

time: 242 us -> 221 us (0.913)
  Pallas kernels: 236 us -> 216 us
    pallas_call x1, Pallas kernels: 236 us -> 216 us  [body(): pl.pallas_call(functools.partial(kernel, n_dp, n_seq), out_shape=(jax.Sha...]
where the time goes in v3:
time: 221 us
  Pallas kernels  216 us (98%)
  local copies, waits for them, and re-layouts  4.77 us (2%)
    pallas_call x1, Pallas kernels, body(): pl.pallas_call(functools.partial(kernel, n_dp, n_seq), out_shape=(jax.Sha...  216 us
    unnamed x10, local copies, waits for them, and re-layouts  4.77 us

profile of v3, /device:TPU:0, one launch (start us, length us, event | category | flops | bytes accessed | tf_op | source)
XLA Modules:
  0.0 221.3 jit_solution(8267819418668703661)
XLA Ops:
  0.6 215.9 %shard_map.93 = (bf16[256,1536]{1,0:T(8,128)(2,1)}, bf16[256,1536]{1,0:T(8,128)(2,1)}, bf16[256,1536]{1,0:T(8,128)(2,1)}, f32[384,384]{1,0:T(8,128)}) custom-call(bf16[256,1536]{1,0:T(8,128)(2,1)} %q.1, bf16[256,1536]{1,0:T(8,128)(2,1)} %k.1, bf16[256,1536]{1,0:T(8,128)(2,1)} %v.1, bf16[256,3072]{1,0:T(8,128)(2,1)} %go.1, bf16[384,384]{1,0:T(8,128)(2,1)} %w.1, ...), custom_call_target="tpu_custom_call" | custom-call | flops 9663676416 | bytes 6291456 | tf_op jit(solution)/shard_map/pallas_call | solution.py:256
  216.5 0.0 copy-start.1
  216.5 0.0 copy-start
  216.6 2.2 copy.14
  218.7 0.0 copy-done.1
  218.7 0.0 copy-start.2
  218.7 0.9 copy.15
  219.6 0.0 copy-done
  219.6 0.9 copy.16
  220.5 0.0 copy-done.2
  220.5 0.8 copy.17
Async XLA Ops:
  216.5 2.2 copy-start.1
  216.5 3.1 %copy-start = (bf16[256,1536]{1,0:T(8,128)(2,1)S(1)}, bf16[256,1536]{1,0:T(8,128)(2,1)}, u32[]{:S(2)}) copy-start(bf16[256,1536]{1,0:T(8,128)(2,1)} %get-tuple-element.10) | copy-start | bytes 2359300
  218.7 1.8 copy-start.2

commit v4 on v3

--- a/solution.py
+++ b/solution.py
@@ -112,7 +112,6 @@
 
     gk_acc[...] = jnp.zeros_like(gk_acc)
     gv_acc[...] = jnp.zeros_like(gv_acc)
-    gw_acc[...] = jnp.zeros_like(gw_acc)
     for i in (0, 1, 2, 4):
         own[i].wait()
 
@@ -153,15 +152,12 @@
             probs = weights * (1.0 / jnp.sum(weights, axis=1, keepdims=True))
             low = probs.astype(jnp.bfloat16)
             ah = mul(low, vh, 1, 0).astype(jnp.bfloat16)
-            att[:, c] = ah
+            att[toks(b), c] = ah
             gv_acc[:, c] += mul(low, gh, 0, 0)
             delta = jnp.sum(gh.astype(jnp.float32) * ah.astype(jnp.float32), axis=1, keepdims=True)
             gs = (probs * (mul(gh, vh, 1, 1) - delta) * scale).astype(jnp.bfloat16)
             oq[toks(b), c] = mul(gs, kh, 1, 0).astype(jnp.bfloat16)
             gk_acc[:, c] += mul(gs, qh, 0, 0)
-        step = min(512, d_out)
-        for f in range(0, d_out, step):
-            gw_acc[f:f + step, :] += mul(gg[b, :, f:f + step], att[...], 0, 0)
 
     @pl.loop(0, 2 * n_seq - 1)
     def _(j):
@@ -194,7 +190,11 @@
         to = lax.rem(me + d, n_seq)
         returned(1, ok, gk, me, to).start()
         returned(2, ov, gv, me, to).start()
-    part[...] = gw_acc[...].astype(jnp.bfloat16)
+    step = min(512, d_out)
+    for f in range(0, d_out, step):
+        total = mul(gg[:, :, f:f + step].reshape(group, step), att[...], 0, 0)
+        gw_acc[f:f + step, :] = total
+        part[f:f + step, :] = total.astype(jnp.bfloat16)
 
     def partial(frm, to):
         return remote(part.at[feats(to), :], recv.at[frm], s_p.at[to], r_p.at[frm], dp=to)
@@ -265,7 +265,7 @@
         + [pltpu.VMEM((group, width), f32)] * 2
         + [pltpu.VMEM((d_out, width), f32), pltpu.VMEM((d_out, width), bf),
            pltpu.VMEM((n_dp, wrows, width), bf),
-           pltpu.VMEM((tok, width), bf), pltpu.VMEM((tok, width), bf)]
+           pltpu.VMEM((group, width), bf), pltpu.VMEM((tok, width), bf)]
         + [dma((3, n_seq)), dma((3, n_seq)), dma((n_dp,)), dma((n_dp,)),
            dma((n_seq,)), dma((n_seq,)), dma((n_seq,)),
            dma((3, n_seq)), dma((3, n_seq)), dma((n_dp,)), dma((n_dp,)), dma((5,))],

time: 221 us -> 221 us (level)
  no operation moved by 1% of the time
where the time goes in v4:
time: 221 us
  Pallas kernels  215 us (97%)
  local copies, waits for them, and re-layouts  4.77 us (2%)
    pallas_call x1, Pallas kernels, body(): pl.pallas_call(functools.partial(kernel, n_dp, n_seq), out_shape=(jax.Sha...  215 us
    unnamed x10, local copies, waits for them, and re-layouts  4.77 us

profile of v4, /device:TPU:0, one launch (start us, length us, event | category | flops | bytes accessed | tf_op | source)
XLA Modules:
  0.0 220.7 jit_solution(10611814581571652591)
XLA Ops:
  0.6 215.3 %shard_map.93 = (bf16[256,1536]{1,0:T(8,128)(2,1)}, bf16[256,1536]{1,0:T(8,128)(2,1)}, bf16[256,1536]{1,0:T(8,128)(2,1)}, f32[384,384]{1,0:T(8,128)}) custom-call(bf16[256,1536]{1,0:T(8,128)(2,1)} %q.1, bf16[256,1536]{1,0:T(8,128)(2,1)} %k.1, bf16[256,1536]{1,0:T(8,128)(2,1)} %v.1, bf16[256,3072]{1,0:T(8,128)(2,1)} %go.1, bf16[384,384]{1,0:T(8,128)(2,1)} %w.1, ...), custom_call_target="tpu_custom_call" | custom-call | flops 9663676416 | bytes 6291456 | tf_op jit(solution)/shard_map/pallas_call | solution.py:256
  216.0 0.0 copy-start.1
  216.0 0.0 copy-start
  216.0 2.2 copy.14
  218.2 0.0 copy-done.1
  218.2 0.0 copy-start.2
  218.2 0.9 copy.15
  219.0 0.0 copy-done
  219.1 0.9 copy.16
  219.9 0.0 copy-done.2
  219.9 0.8 copy.17
Async XLA Ops:
  216.0 2.2 copy-start.1
  216.0 3.1 %copy-start = (bf16[256,1536]{1,0:T(8,128)(2,1)S(1)}, bf16[256,1536]{1,0:T(8,128)(2,1)}, u32[]{:S(2)}) copy-start(bf16[256,1536]{1,0:T(8,128)(2,1)} %get-tuple-element.10) | copy-start | bytes 2359300
  218.2 1.8 copy-start.2
